TPU v7x, 32 devices: a whole 2x2x4 slice. The times are simulated.
32 devices in a mesh: grp: 4 (over z), mem: 8 (over y, x, core).
Axes of the slice: x: 2, y: 2, z: 4, core: 2. Of those that a mesh axis runs over, the one named last changes fastest.
Arguments:
- embeddings: bfloat16 [12288, 1024], P(('grp', 'mem')), may hold values from -6 to 6
- row_target: int32 [12288, 1], P(('grp', 'mem')), may hold values from 0 to 31; in each aligned block of 384 rows (0 to 383, 384 to 767, ...) at most 24 rows name the same one
Outputs:
- best_cosine: float32 [12288], P(('grp', 'mem'))
Inputs may be any that keep to these rules, and one draw needn't show every extreme that they name: `row_target`: among the rows of one device no owner device is named by more than 24 rows, a bound that some block reaches.
All inputs are finite; a program needn't handle non-finite values.
Results may differ from a plain program's by a relative error of at most 0.0012.
Values may be sent and summed in bfloat16 or wider, within the bound.
A program may use at most 128 MiB of HBM per device.

v0:
```python
import math

import jax
import jax.numpy as jnp
from jax import lax
from jax.sharding import PartitionSpec as P


def normalize(embeddings):
    values = embeddings.astype(jnp.float32)
    width = embeddings.shape[1]
    inv_norm = lax.rsqrt(jnp.mean(values * values, axis=1, keepdims=True) + 1e-06) * (
        1.0 / math.sqrt(width)
    )
    return (values * inv_norm).astype(jnp.bfloat16)


def cross_cosines(left_rows, right_rows):
    return lax.dot_general(
        left_rows, right_rows, (((1,), (1,)), ((), ())), preferred_element_type=jnp.float32
    )


def per_device(embeddings, row_target):
    row_count = embeddings.shape[0]
    groups = lax.axis_size("grp")
    members = lax.axis_size("mem")
    devices = groups * members
    capacity = 2 * row_count // devices
    slots = devices * capacity
    unit_rows = normalize(embeddings)
    target = row_target[:, 0]
    onehot = (target[:, None] == jnp.arange(devices, dtype=jnp.int32)[None, :]).astype(jnp.int32)
    slot_index = jnp.sum(onehot * jnp.cumsum(onehot, axis=0), axis=1) - 1
    position = target * capacity + slot_index
    placing = (position[:, None] == jnp.arange(slots, dtype=jnp.int32)[None, :]).astype(
        jnp.bfloat16
    )
    send_rows = lax.dot_general(
        placing, unit_rows, (((0,), (0,)), ((), ())), preferred_element_type=jnp.float32
    ).astype(jnp.bfloat16)
    send_flags = jnp.sum(placing.astype(jnp.float32), axis=0).astype(jnp.bfloat16)
    held_rows, held_flags = (
        lax.all_to_all(send_rows, ("grp", "mem"), split_axis=0, concat_axis=0, tiled=True),
        lax.all_to_all(send_flags, ("grp", "mem"), split_axis=0, concat_axis=0, tiled=True),
    )
    own_offset = lax.axis_index("mem") * slots
    own_column = own_offset + jnp.arange(slots, dtype=jnp.int32)
    piece_rows = lax.all_gather(held_rows, "mem", axis=0, tiled=True)
    piece_flags = lax.all_gather(held_flags, "mem", axis=0, tiled=True)
    cosines = cross_cosines(held_rows, piece_rows)
    column = jnp.arange(piece_rows.shape[0], dtype=jnp.int32)
    keep_mask = (piece_flags[None, :] > 0) & (column[None, :] != own_column[:, None])
    best_value = jnp.maximum(
        jnp.full((slots,), -1.0, jnp.float32), jnp.max(jnp.where(keep_mask, cosines, -1.0), axis=1)
    )
    came_back = lax.all_to_all(best_value, ("grp", "mem"), split_axis=0, concat_axis=0, tiled=True)
    return jnp.sum(placing.astype(jnp.float32) * came_back[None, :], axis=1)


def solution(mesh):
    in_specs = (P(("grp", "mem"), None), P(("grp", "mem"), None))
    out_specs = P(("grp", "mem"))
    return jax.shard_map(
        per_device, mesh=mesh, in_specs=in_specs, out_specs=out_specs, check_vma=False
    )
```

profile of v0, /device:TPU:0, one launch (start us, length us, event | category | flops | bytes accessed | tf_op | source)
XLA Modules:
  0.0 164.1 jit_solution(14646108263430087224)
XLA Ops:
  6.5 1.4 fusion.1
  7.9 0.7 reduce.1
  8.6 0.9 reduce-window.6
  9.5 0.2 slice_reduce_fusion
  9.8 0.1 fusion.9
  9.9 0.7 add_reduce_fusion
  10.6 2.3 %convolution_convert_fusion = bf16[768,1024]{1,0:T(8,128)(2,1)S(1)} fusion(bf16[384,1024]{1,0:T(8,128)(2,1)} %param.2, f32[384]{0:T(512)S(1)} %rsqrt_multiply_fusion, s32[384]{0:T(512)S(1)} %add_reduce_fusion), kind=kOutput, calls=%fused_computation.5 | convolution fusion | flops 606240768 | bytes 2362368 | tf_op jit(solution)/shard_map/dot_general | solution.py:39
  12.8 45.2 %all_to_all.31 = bf16[32,24,1024]{2,1,0:T(8,128)(2,1)} all-to-all(bf16[32,24,1024]{2,1,0:T(8,128)(2,1)S(1)} %bitcast.25), channel_id=1, replica_groups=mesh['grp'=4,'mem'=8] {'grp','mem'}, dimensions={0} | all-to-all | bytes 3145728 | tf_op jit(solution)/shard_map/all_to_all | solution.py:44
  58.1 0.2 fusion.4
  58.3 0.7 all_to_all.27
  59.0 3.1 %all-to-all-start = ((bf16[32,24,1]{1,2,0:T(2,128)(2,1)}), bf16[32,24,1]{1,2,0:T(2,128)(2,1)S(1)}, u32[]{:S(2)}, u32[]{:S(2)}) async-start(bf16[32,24,1]{1,2,0:T(2,128)(2,1)} %all_to_all.27), calls=%async_computation | async-start | bytes 32768 | tf_op jit(solution)/shard_map/all_to_all | solution.py:45
  62.1 7.1 %all-to-all-done = bf16[32,24,1]{1,2,0:T(2,128)(2,1)S(1)} async-done(((bf16[32,24,1]{1,2,0:T(2,128)(2,1)}), bf16[32,24,1]{1,2,0:T(2,128)(2,1)S(1)}, u32[]{:S(2)}, u32[]{:S(2)}) %all-to-all-start) | async-done | bytes 1568 | tf_op jit(solution)/shard_map/all_to_all | solution.py:45
  69.2 0.1 reduce.5
  69.3 0.1 reshape.62
  69.4 8.2 %all-gather = bf16[8,1,768]{2,1,0:T(2,128)(2,1)S(1)} all-gather(bf16[1,1,768]{2,1,0:T(2,128)(2,1)S(1)} %reshape.62), channel_id=1, replica_groups=mesh['grp'=4,'mem'=8] {'mem'}, dimensions={0}, use_global_device_ids=true | all-gather | bytes 13824 | tf_op jit(solution)/shard_map/all_gather | solution.py:50
  77.5 0.1 compare_reduce_fusion
  77.7 51.3 %all-gather.3.cloned.1.call-done = bf16[6144,1024]{1,0:T(8,128)(2,1)} async-done(((bf16[768,1024]{1,0:T(8,128)(2,1)}), bf16[6144,1024]{1,0:T(8,128)(2,1)}) %all-gather.3.cloned.1.call-update) | async-done | bytes 12582928 | tf_op jit(solution)/shard_map/all_gather | solution.py:49
  128.9 14.5 %select_reduce_fusion = f32[768]{0:T(1024)S(1)} fusion(bf16[768,1024]{1,0:T(8,128)(2,1)S(1)} %bitcast.24, bf16[6144,1024]{1,0:T(8,128)(2,1)} %all-gather.3.cloned.1.call-done, s32[768]{0:T(1024)S(1)} %iota_add_fusion, pred[6144]{0:T(1024)(128)(4,1)S(1)} %reshape.65), kind=kOutput, calls=%fused_computation | convolution fusion | flops 9682549760 | bytes 14168064 | tf_op jit(solution)/shard_map/dot_general | solution.py:19
  143.4 0.1 max_broadcast_in_dim.14
  143.5 11.6 %all_to_all.32 = f32[32,24,1]{1,2,0:T(1,128)S(1)} all-to-all(f32[32,24,1]{1,2,0:T(1,128)S(1)} %bitcast.26), channel_id=1, replica_groups=mesh['grp'=4,'mem'=8] {'grp','mem'}, dimensions={0} | all-to-all | bytes 6144 | tf_op jit(solution)/shard_map/all_to_all | solution.py:57
  155.1 0.5 broadcast.76
  155.6 0.7 reduce.13
  156.3 0.1 mul.54
  156.3 0.9 multiply_reduce_fusion
  (11 shorter events, 0.1 us)
Async XLA Ops:
  6.5 122.4 %all-gather.3.cloned.1.call-start = ((), (), s32[]{:S(2)}) async-start(), calls=%async_computation.3 | async-start | bytes 14155776 | tf_op jit(solution)/shard_map/all_gather | solution.py:49
  58.1 70.9 %copy-start = (bf16[32,24,1024]{2,1,0:T(8,128)(2,1)S(1)}, bf16[32,24,1024]{2,1,0:T(8,128)(2,1)}, u32[]{:S(2)}) copy-start(bf16[32,24,1024]{2,1,0:T(8,128)(2,1)} %all_to_all.31) | copy-start | bytes 4718596
  59.0 10.2 %all-to-all-start = ((bf16[32,24,1]{1,2,0:T(2,128)(2,1)}), bf16[32,24,1]{1,2,0:T(2,128)(2,1)S(1)}, u32[]{:S(2)}, u32[]{:S(2)}) async-start(bf16[32,24,1]{1,2,0:T(2,128)(2,1)} %all_to_all.27), calls=%async_computation | async-start | bytes 32768 | tf_op jit(solution)/shard_map/all_to_all | solution.py:45
Sparse Core Ops, SparseCore 0:
  58.2 70.6 all-gather.2
where the time goes:
time: 164 us
  blocking collectives  64.9 us (40%)
  waiting for transfers between devices  58.4 us (36%)
  matrix products  16.7 us (10%)
  between operations  13.5 us (8%)
  other arithmetic  5.75 us (4%)
  starting transfers between devices  3.08 us (2%)
  local copies, waits for them, and re-layouts  1.73 us (1%)
    all_gather x1, waiting for transfers between devices, per_device(): piece_rows = lax.all_gather(held_rows, 'mem', axis=0, tiled=True)  51.3 us
    all_to_all x1, blocking collectives, per_device(): lax.all_to_all(send_rows, ('grp', 'mem'), split_axis=0, concat_axis=0, ti...  45.2 us
    dot_general x1, matrix products, cross_cosines(): lax.dot_general(left_rows, right_rows, (((1,), (1,)), ((), ())), preferre...  14.5 us
    all_to_all x1, blocking collectives, per_device(): lax.all_to_all(best_value, ('grp', 'mem'), split_axis=0, concat_axis=0, t...  11.6 us
    all_gather x1, blocking collectives, per_device(): piece_flags = lax.all_gather(held_flags, 'mem', axis=0, tiled=True)  8.15 us
    all_to_all x1, waiting for transfers between devices, per_device(): lax.all_to_all(send_flags, ('grp', 'mem'), split_axis=0, concat_axis=0, t...  7.13 us
  transfers between devices with their start and end apart: 2, of which 2 were waited for; matrix products, arithmetic and copies ran while one was open for 0% of the time, Pallas kernels for 0%

commit v1 on v0

v1 whole, which is shorter than its diff:
```python
import functools
import math

import jax
import jax.numpy as jnp
from jax import lax
from jax.experimental import pallas as pl
from jax.experimental.pallas import tpu as pltpu
from jax.sharding import PartitionSpec as P

MESH = pl.DeviceIdType.MESH
LANES = 128
TAG = 16


def kernel(
    groups, members, emb_ref, target_ref, out_ref,
    plane, line, seen, plane_out, line_out, plane_in, line_in, own_best, line_best,
    ring_send, ring_recv, pass_send, line_send, line_recv,
    back_send, back_recv, home_send, home_recv,
):
    rows, width = emb_ref.shape
    half = members // 2
    g, m = lax.axis_index("grp"), lax.axis_index("mem")
    full = (groups - 1) // 2
    has_half = groups % 2 == 0
    steps = list(range(1, full + 1)) + ([groups // 2] if has_half else [])
    lines = len(steps)

    def partner_of(i):
        return i + 1 - 2 * lax.rem(i, 2)

    if has_half:
        low = lax.rem(g, groups // 2)
        upper = g // (groups // 2)
        takes_half = lax.rem(low + upper, 2) == 1
        gives_half = lax.rem(low + upper, 2) == 0

    def if_takes(j, body):
        if j < full:
            body()
        else:
            pl.when(takes_half)(body)

    def if_gives(j, body):
        if j < full:
            body()
        else:
            pl.when(gives_half)(body)

    barrier = pltpu.get_barrier_semaphore()
    for i in range(1, members):
        pl.semaphore_signal(
            barrier, inc=1, device_id=(g, lax.rem(m + i, members)), device_id_type=MESH
        )
    for i in range(1, groups):
        pl.semaphore_signal(
            barrier, inc=1, device_id=(lax.rem(g + i, groups), m), device_id_type=MESH
        )

    values = emb_ref[...].astype(jnp.float32)
    inv_norm = lax.rsqrt(jnp.mean(values * values, axis=1, keepdims=True) + 1e-06) * (
        1.0 / math.sqrt(width)
    )
    plane[0, pl.ds(0, rows), :] = (values * inv_norm).astype(jnp.bfloat16)
    cluster = jnp.floor((target_ref[...].astype(jnp.float32) + 0.5) * (1.0 / members))
    plane[0, pl.ds(rows, TAG), :] = jnp.zeros((TAG, width), jnp.bfloat16)
    plane[0, pl.ds(rows, TAG), pl.ds(0, rows)] = jnp.broadcast_to(cluster, (TAG, rows)).astype(
        jnp.bfloat16
    )

    pl.semaphore_wait(barrier, members - 1 + groups - 1)

    def line_copy(j):
        return pltpu.make_async_remote_copy(
            src_ref=plane.at[0], dst_ref=line.at[j],
            send_sem=line_send.at[j], recv_sem=line_recv.at[j],
            device_id=(lax.rem(g + groups - steps[j], groups), m), device_id_type=MESH,
        )

    def ring_copy(s):
        return pltpu.make_async_remote_copy(
            src_ref=plane.at[0], dst_ref=plane.at[2 * s],
            send_sem=ring_send.at[s], recv_sem=ring_recv.at[2 * s],
            device_id=(g, lax.rem(m + members - 2 * s, members)), device_id_type=MESH,
        )

    def pass_copy(s):
        return pltpu.make_async_remote_copy(
            src_ref=plane.at[2 * s], dst_ref=plane.at[2 * s + 1],
            send_sem=pass_send.at[s], recv_sem=ring_recv.at[2 * s + 1],
            device_id=(g, partner_of(m)), device_id_type=MESH,
        )

    for j in range(lines):
        if_gives(j, lambda j=j: line_copy(j).start())
    for s in range(1, half):
        ring_copy(s).start()
    pass_copy(0).start()

    def cluster_row(ref, i):
        return ref[i, pl.ds(rows, TAG), pl.ds(0, rows)].astype(jnp.float32)[0:1, :]

    def cluster_columns(i):
        seen[...] = jnp.transpose(jnp.broadcast_to(cluster_row(plane, i), (LANES, rows)))

    def cosines(i, left):
        return lax.dot_general(
            plane[i, pl.ds(0, rows), :], left, (((1,), (1,)), ((), ())),
            preferred_element_type=jnp.float32,
        )

    def masked(cos, across, k, same):
        part = cos[:, k * LANES:(k + 1) * LANES]
        keep = seen[...] == across[:, k * LANES:(k + 1) * LANES]
        if same:
            down = lax.broadcasted_iota(jnp.int32, (rows, LANES), 0)
            over = lax.broadcasted_iota(jnp.int32, (rows, LANES), 1) + k * LANES
            keep = keep & (down != over)
        return jnp.where(keep, part, -1.0)

    own_best[...] = jnp.full((8, rows), -1.0, jnp.float32)
    line_best[...] = jnp.full((lines, 8, rows), -1.0, jnp.float32)

    def own_pairs(i, same=False):
        cluster_columns(i)
        cos = cosines(i, plane[0, pl.ds(0, rows), :])
        across = cluster_row(plane, 0)
        for k in range(rows // LANES):
            at = pl.ds(k * LANES, LANES)
            best = jnp.max(masked(cos, across, k, same), axis=0, keepdims=True)
            own_best[:, at] = jnp.maximum(own_best[:, at], best)

    own_pairs(0, True)

    def even(s, carry):
        ring_copy(s).wait_recv()
        pass_copy(s).start()
        own_pairs(2 * s)
        return carry

    def odd(s, carry):
        pass_copy(s).wait_recv()
        own_pairs(2 * s + 1)
        return carry

    lax.fori_loop(1, half, even, 0)
    lax.fori_loop(0, half, odd, 0)

    for j in range(lines):
        if_takes(j, lambda j=j: line_copy(j).wait_recv())

    def line_pairs(j, i, reached):
        cos = cosines(i, line[j, pl.ds(0, rows), :])
        across = cluster_row(line, j)
        for k in range(rows // LANES):
            at = pl.ds(k * LANES, LANES)
            part = masked(cos, across, k, False)
            line_best[j, :, at] = jnp.maximum(
                line_best[j, :, at], jnp.max(part, axis=0, keepdims=True)
            )
            reached[...] = jnp.maximum(reached[...], part)

    def back_copy(i):
        above = lax.rem(m + 2 * (i // 2), members)
        holder = lax.rem(i, 2) * partner_of(above) + (1 - lax.rem(i, 2)) * above
        return pltpu.make_async_remote_copy(
            src_ref=plane_out.at[i], dst_ref=plane_in.at[i],
            send_sem=back_send.at[i], recv_sem=back_recv.at[i],
            device_id=(g, holder), device_id_type=MESH,
        )

    def home_copy(j):
        return pltpu.make_async_remote_copy(
            src_ref=line_out.at[j], dst_ref=line_in.at[j],
            send_sem=home_send.at[j], recv_sem=home_recv.at[j],
            device_id=(lax.rem(g + steps[j], groups), m), device_id_type=MESH,
        )

    def across_lines(i, reached):
        cluster_columns(i)
        reached[...] = jnp.full((rows, LANES), -1.0, jnp.float32)
        for j in range(lines):
            if_takes(j, lambda j=j: line_pairs(j, i, reached))
        best = jnp.max(jnp.transpose(reached[...]), axis=0, keepdims=True)
        plane_out[i] = jnp.broadcast_to(best, (8, rows))

    def with_reached(reached):
        def step(i, carry):
            across_lines(i, reached)
            back_copy(i).start()
            return carry

        lax.fori_loop(1, members, step, 0)
        across_lines(0, reached)

    pl.run_scoped(with_reached, pltpu.VMEM((rows, LANES), jnp.float32))

    def send_home(j):
        line_out[j] = line_best[j]
        home_copy(j).start()

    for j in range(lines):
        if_takes(j, lambda j=j: send_home(j))

    own_best[...] = jnp.maximum(own_best[...], plane_out[0])

    def collect(i, carry):
        back_copy(i).wait_recv()
        own_best[...] = jnp.maximum(own_best[...], plane_in[i])
        return carry

    lax.fori_loop(1, members, collect, 0)

    def collect_home(j):
        home_copy(j).wait_recv()
        own_best[...] = jnp.maximum(own_best[...], line_in[j])

    for j in range(lines):
        if_gives(j, lambda j=j: collect_home(j))
    out_ref[...] = own_best[0:1, :]

    for j in range(lines):
        if_gives(j, lambda j=j: line_copy(j).wait_send())
        if_takes(j, lambda j=j: home_copy(j).wait_send())
    for s in range(half):
        if s > 0:
            ring_copy(s).wait_send()
        pass_copy(s).wait_send()
    for i in range(1, members):
        back_copy(i).wait_send()


def per_device(embeddings, row_target):
    rows, width = embeddings.shape
    groups = lax.axis_size("grp")
    members = lax.axis_size("mem")
    lines = groups // 2
    block = (rows + TAG, width)
    dma = pltpu.SemaphoreType.DMA
    f32 = jnp.float32
    best = pl.pallas_call(
        functools.partial(kernel, groups, members),
        out_shape=jax.ShapeDtypeStruct((1, rows), f32),
        in_specs=[pl.BlockSpec(memory_space=pltpu.VMEM)] * 2,
        out_specs=pl.BlockSpec(memory_space=pltpu.VMEM),
        scratch_shapes=[
            pltpu.VMEM((members, *block), jnp.bfloat16),
            pltpu.VMEM((lines, *block), jnp.bfloat16),
            pltpu.VMEM((rows, LANES), f32),
            pltpu.VMEM((members, 8, rows), f32),
            pltpu.VMEM((lines, 8, rows), f32),
            pltpu.VMEM((members, 8, rows), f32),
            pltpu.VMEM((lines, 8, rows), f32),
            pltpu.VMEM((8, rows), f32),
            pltpu.VMEM((lines, 8, rows), f32),
            dma((members // 2,)),
            dma((members,)),
            dma((members // 2,)),
            dma((lines,)),
            dma((lines,)),
            dma((members,)),
            dma((members,)),
            dma((lines,)),
            dma((lines,)),
        ],
        compiler_params=pltpu.CompilerParams(
            collective_id=0, has_side_effects=True, vmem_limit_bytes=48 * 2**20
        ),
    )(embeddings, row_target.reshape(1, rows))
    return best.reshape(rows)


def solution(mesh):
    in_specs = (P(("grp", "mem"), None), P(("grp", "mem"), None))
    return jax.shard_map(
        per_device, mesh=mesh, in_specs=in_specs, out_specs=P(("grp", "mem")), check_vma=False
    )
```

time: 164 us -> 62 us (0.38)
  blocking collectives: 64.9 us -> 0 us
  Pallas kernels: 0 us -> 59.4 us
  waiting for transfers between devices: 58.4 us -> 0 us
  matrix products: 16.7 us -> 0 us
  between operations: 13.5 us -> 0.01 us
  other arithmetic: 5.75 us -> 0.6 us
  starting transfers between devices: 3.08 us -> 0 us
    pallas_call x0 -> x1, Pallas kernels: none -> 59.4 us  [per_device(): pl.pallas_call(functools.partial(kernel, groups, members), out_shape=jax....]
    all_to_all x2 -> x0, blocking collectives: 56.8 us -> none  [the longest x1 45.2 us: per_device(): lax.all_to_all(send_rows, ('grp', 'mem'), split_axis=0, concat_axis=0, ti...]
    all_gather x1 -> x0, waiting for transfers between devices: 51.3 us -> none  [per_device(): piece_rows = lax.all_gather(held_rows, 'mem', axis=0, tiled=True)]
    dot_general x2 -> x0, matrix products: 16.7 us -> none  [the longest x1 14.5 us: cross_cosines(): lax.dot_general(left_rows, right_rows, (((1,), (1,)), ((), ())), preferre...]
    all_gather x1 -> x0, blocking collectives: 8.15 us -> none  [per_device(): piece_flags = lax.all_gather(held_flags, 'mem', axis=0, tiled=True)]
    all_to_all x1 -> x0, waiting for transfers between devices: 7.13 us -> none  [per_device(): lax.all_to_all(send_flags, ('grp', 'mem'), split_axis=0, concat_axis=0, t...]
    all_to_all x1 -> x0, starting transfers between devices: 3.08 us -> none  [per_device(): lax.all_to_all(send_flags, ('grp', 'mem'), split_axis=0, concat_axis=0, t...]
    reduce_sum x4 -> x0, other arithmetic: 2.57 us -> none  [the longest x1 1.37 us: normalize(): jnp.mean(values * values, axis=1, keepdims=True) + 1e-06]
  transfers between devices with their start and end apart: 2 -> 0, of which waited for: 2 -> 0; matrix products, arithmetic and copies ran while one was open for 0% -> 0% of each run, Pallas kernels for 0% -> 0%
where the time goes in v1:
time: 62 us; the launch traced here: 61.8 us
  Pallas kernels  59.4 us (96%)
  local copies, waits for them, and re-layouts  1.81 us (3%)
    pallas_call x1, Pallas kernels, per_device(): pl.pallas_call(functools.partial(kernel, groups, members), out_shape=jax....  59.4 us
    unnamed x4, local copies, waits for them, and re-layouts  1.81 us

profile of v1, /device:TPU:0, one launch (start us, length us, event | category | flops | bytes accessed | tf_op | source)
XLA Modules:
  0.0 61.8 jit_solution(13939013526383968803)
XLA Ops:
  0.0 0.0 copy-start.1
  0.0 0.7 %copy-done.1 = s32[384,1]{0,1:T(1,128)S(1)} copy-done((s32[384,1]{0,1:T(1,128)S(1)}, s32[384,1]{0,1:T(1,128)}, u32[]{:S(2)}) %copy-start.1) | copy-done | bytes 1560
  0.7 0.0 copy-start
  0.7 1.1 %copy-done = bf16[384,1024]{1,0:T(8,128)(2,1)S(1)} copy-done((bf16[384,1024]{1,0:T(8,128)(2,1)S(1)}, bf16[384,1024]{1,0:T(8,128)(2,1)}, u32[]{:S(2)}) %copy-start) | copy-done | bytes 786456
  1.8 59.4 %shard_map.28 = f32[1,384]{1,0:T(1,128)S(1)} custom-call(bf16[384,1024]{1,0:T(8,128)(2,1)S(1)} %copy-done, s32[1,384]{1,0:T(1,128)S(1)} %bitcast.1), custom_call_target="tpu_custom_call" | custom-call | tf_op jit(solution)/shard_map/pallas_call | solution.py:242
  61.2 0.6 reduce
Async XLA Ops:
  0.0 0.7 %copy-start.1 = (s32[384,1]{0,1:T(1,128)S(1)}, s32[384,1]{0,1:T(1,128)}, u32[]{:S(2)}) copy-start(s32[384,1]{0,1:T(1,128)} %param.3) | copy-start | bytes 4612
  0.7 1.1 %copy-start = (bf16[384,1024]{1,0:T(8,128)(2,1)S(1)}, bf16[384,1024]{1,0:T(8,128)(2,1)}, u32[]{:S(2)}) copy-start(bf16[384,1024]{1,0:T(8,128)(2,1)} %emb_ref.1) | copy-start | bytes 2359300

commit v2 on v1

v2 whole, which is shorter than its diff:
```python
import functools
import math

import jax
import jax.numpy as jnp
from jax import lax
from jax.experimental import pallas as pl
from jax.experimental.pallas import tpu as pltpu
from jax.sharding import PartitionSpec as P

MESH = pl.DeviceIdType.MESH
LANES = 128
SUBLANES = 8


def xor(a, b, count):
    total, bit = 0, 1
    while bit < count:
        one, other = lax.rem(a // bit, 2), (b // bit) % 2
        total = total + bit * (one + other - 2 * one * other)
        bit *= 2
    return total


def kernel(
    groups, members, emb_ref, target_ref, out_ref,
    plane, line, plane_tag, line_tag, seen, reached, plane_out, line_out, plane_in, line_in, own_best,
    ring_send, ring_recv, line_send, line_recv,
    tag_send, tag_recv, end_send, end_recv,
    back_send, back_recv, home_send, home_recv,
):
    rows, width = emb_ref.shape
    pieces = rows // LANES
    g, m = lax.axis_index("grp"), lax.axis_index("mem")
    full = (groups - 1) // 2
    has_half = groups % 2 == 0
    steps = list(range(1, full + 1)) + ([groups // 2] if has_half else [])
    lines = len(steps)
    halves = [pl.ds(0, rows // 2), pl.ds(rows // 2, rows // 2)]
    parts = [(0, pieces - 1), (pieces - 1, pieces)]
    relayed = members == 8

    if has_half:
        low = lax.rem(g, groups // 2)
        upper = g // (groups // 2)
        takes_half = lax.rem(low + upper, 2) == 1
        gives_half = lax.rem(low + upper, 2) == 0

    def if_takes(j, body):
        if j < full:
            body()
        else:
            pl.when(takes_half)(body)

    def if_gives(j, body):
        if j < full:
            body()
        else:
            pl.when(gives_half)(body)

    def member(i):
        return (g, xor(m, i, members))

    def group_below(j):
        return (lax.rem(g + groups - steps[j], groups), m)

    barrier = pltpu.get_barrier_semaphore()
    for i in range(1, members):
        pl.semaphore_signal(barrier, inc=1, device_id=member(i), device_id_type=MESH)
    for i in range(1, groups):
        pl.semaphore_signal(
            barrier, inc=1, device_id=(lax.rem(g + i, groups), m), device_id_type=MESH
        )

    values = emb_ref[...].astype(jnp.float32)
    inv_norm = lax.rsqrt(jnp.mean(values * values, axis=1, keepdims=True) + 1e-06) * (
        1.0 / math.sqrt(width)
    )
    plane[0] = (values * inv_norm).astype(jnp.bfloat16)
    cluster = jnp.floor((target_ref[...].astype(jnp.float32) + 0.5) * (1.0 / members))
    plane_tag[0] = jnp.zeros((SUBLANES, LANES), jnp.float32)
    for k in range(pieces):
        plane_tag[0, k:k + 1, :] = cluster[:, k * LANES:(k + 1) * LANES]

    pl.semaphore_wait(barrier, members - 1 + groups - 1)

    def line_copy(j, p):
        at = pl.ds(parts[p][0] * LANES, (parts[p][1] - parts[p][0]) * LANES)
        return pltpu.make_async_remote_copy(
            src_ref=plane.at[0, at], dst_ref=line.at[j, at],
            send_sem=line_send.at[j, p], recv_sem=line_recv.at[j, p],
            device_id=group_below(j), device_id_type=MESH,
        )

    def plane_copy(held, to, h):
        slot = held ^ to
        return pltpu.make_async_remote_copy(
            src_ref=plane.at[held, halves[h]], dst_ref=plane.at[slot, halves[h]],
            send_sem=ring_send.at[slot, h], recv_sem=ring_recv.at[slot, h],
            device_id=member(to), device_id_type=MESH,
        )

    def tag_copy(i):
        return pltpu.make_async_remote_copy(
            src_ref=plane_tag.at[0], dst_ref=plane_tag.at[i],
            send_sem=tag_send.at[i], recv_sem=tag_recv.at[i],
            device_id=member(i), device_id_type=MESH,
        )

    def end_copy(j):
        return pltpu.make_async_remote_copy(
            src_ref=plane_tag.at[0], dst_ref=line_tag.at[j],
            send_sem=end_send.at[j], recv_sem=end_recv.at[j],
            device_id=group_below(j), device_id_type=MESH,
        )

    plan = {}
    for slot in range(2, members, 2):
        for h in range(2):
            plan[slot, h] = (0, slot)
    if relayed:
        order = [(2, 0), (4, 1), (2, 1), (4, 0), (6, 0), (6, 1)]
        plan[6, 0], plan[6, 1] = (2, 4), (4, 2)
    else:
        order = [(slot, h) for slot in range(2, members, 2) for h in range(2)]

    for i in range(1, members):
        tag_copy(i).start()
    for j in range(lines):
        if_gives(j, lambda j=j: end_copy(j).start())
    first = [key for key in order if plan[key][0] == 0]
    for p in range(2):
        for h, to in [(h, to) for to, h in first[p * len(first) // 2:(p + 1) * len(first) // 2]]:
            plane_copy(0, to, h).start()
        for j in range(lines):
            if_gives(j, lambda j=j, p=p: line_copy(j, p).start())
    for h in range(2):
        plane_copy(0, 1, h).start()

    def see(i):
        for k in range(pieces):
            row = jnp.broadcast_to(plane_tag[i, k:k + 1, :], (LANES, LANES))
            seen[k * LANES:(k + 1) * LANES, :] = jnp.transpose(row)

    def cosines(i, left):
        return lax.dot_general(
            plane[i], left, (((1,), (1,)), ((), ())), preferred_element_type=jnp.float32
        )

    own_best[...] = jnp.full((SUBLANES, rows), -1.0, jnp.float32)
    line_out[...] = jnp.full((lines, SUBLANES, rows), -1.0, jnp.float32)
    plane_out[...] = jnp.full((members, SUBLANES, rows), -1.0, jnp.float32)

    def own_pairs(i, same=False):
        see(i)
        cos = cosines(i, plane[0])
        for k in range(pieces):
            at = pl.ds(k * LANES, LANES)
            keep = seen[...] == plane_tag[0, k:k + 1, :]
            if same:
                down = lax.broadcasted_iota(jnp.int32, (rows, LANES), 0)
                over = lax.broadcasted_iota(jnp.int32, (rows, LANES), 1) + k * LANES
                keep = keep & (down != over)
            part = jnp.where(keep, cos[:, k * LANES:(k + 1) * LANES], -1.0)
            own_best[:, at] = jnp.maximum(own_best[:, at], jnp.max(part, axis=0, keepdims=True))

    own_pairs(0, True)
    for i in range(1, members):
        tag_copy(i).wait_recv()
    for j in range(lines):
        if_takes(j, lambda j=j: end_copy(j).wait_recv())

    def arrive(slot, h):
        held, to = plan[slot, h]
        plane_copy(held, to, h).wait_recv()
        for key, (source, onto) in plan.items():
            if source == slot and key[1] == h:
                plane_copy(source, onto, h).start()
        plane_copy(slot, 1, h).start()

    for h in range(2):
        plane_copy(0, 1, h).wait_recv()
    own_pairs(1)
    have = 0
    for slot, h in order:
        arrive(slot, h)
        if slot == 4 and h == 0 and relayed:
            for i in (2, 4):
                own_pairs(i)
            have = 4
    for i in range(2, members):
        if i % 2:
            for h in range(2):
                plane_copy(i - 1, 1, h).wait_recv()
        if not (have and i in (2, 4)):
            own_pairs(i)

    def line_pairs(j, i, p):
        start, stop = parts[p]
        cos = cosines(i, line[j, start * LANES:stop * LANES, :])
        for k in range(start, stop):
            at = pl.ds(k * LANES, LANES)
            keep = seen[...] == line_tag[j, k:k + 1, :]
            cut = cos[:, (k - start) * LANES:(k - start + 1) * LANES]
            part = jnp.where(keep, cut, -1.0)
            line_out[j, :, at] = jnp.maximum(
                line_out[j, :, at], jnp.max(part, axis=0, keepdims=True)
            )
            reached[...] = jnp.maximum(reached[...], part)

    def back_copy(i):
        return pltpu.make_async_remote_copy(
            src_ref=plane_out.at[i], dst_ref=plane_in.at[i],
            send_sem=back_send.at[i], recv_sem=back_recv.at[i],
            device_id=member(i), device_id_type=MESH,
        )

    def home_copy(j):
        return pltpu.make_async_remote_copy(
            src_ref=line_out.at[j], dst_ref=line_in.at[j],
            send_sem=home_send.at[j], recv_sem=home_recv.at[j],
            device_id=(lax.rem(g + steps[j], groups), m), device_id_type=MESH,
        )

    def across_lines(i, p):
        see(i)
        reached[...] = jnp.full((rows, LANES), -1.0, jnp.float32)
        for j in range(lines):
            if_takes(j, lambda j=j: line_pairs(j, i, p))
        best = jnp.max(jnp.transpose(reached[...]), axis=0, keepdims=True)
        plane_out[i] = jnp.maximum(plane_out[i], best)

    for p in range(2):
        for j in range(lines):
            if_takes(j, lambda j=j, p=p: line_copy(j, p).wait_recv())

        def step(i, carry, p=p):
            across_lines(i, p)
            if p == 1:
                back_copy(i).start()
            return carry

        lax.fori_loop(1, members, step, 0)
        across_lines(0, p)

    for j in range(lines):
        if_takes(j, lambda j=j: home_copy(j).start())

    own_best[...] = jnp.maximum(own_best[...], plane_out[0])

    def collect(i, carry):
        back_copy(i).wait_recv()
        own_best[...] = jnp.maximum(own_best[...], plane_in[i])
        return carry

    lax.fori_loop(1, members, collect, 0)

    def collect_home(j):
        home_copy(j).wait_recv()
        own_best[...] = jnp.maximum(own_best[...], line_in[j])

    for j in range(lines):
        if_gives(j, lambda j=j: collect_home(j))
    out_ref[...] = own_best[0:1, :]

    for j in range(lines):
        for p in range(2):
            if_gives(j, lambda j=j, p=p: line_copy(j, p).wait_send())
        if_gives(j, lambda j=j: end_copy(j).wait_send())
        if_takes(j, lambda j=j: home_copy(j).wait_send())
    for h in range(2):
        for slot in range(2, members, 2):
            plane_copy(*plan[slot, h], h).wait_send()
        for slot in range(0, members, 2):
            plane_copy(slot, 1, h).wait_send()
    for i in range(1, members):
        tag_copy(i).wait_send()
        back_copy(i).wait_send()


def per_device(embeddings, row_target):
    rows, width = embeddings.shape
    groups = lax.axis_size("grp")
    members = lax.axis_size("mem")
    lines = groups // 2
    dma = pltpu.SemaphoreType.DMA
    f32 = jnp.float32
    best = pl.pallas_call(
        functools.partial(kernel, groups, members),
        out_shape=jax.ShapeDtypeStruct((1, rows), f32),
        in_specs=[pl.BlockSpec(memory_space=pltpu.VMEM)] * 2,
        out_specs=pl.BlockSpec(memory_space=pltpu.VMEM),
        scratch_shapes=[
            pltpu.VMEM((members, rows, width), jnp.bfloat16),
            pltpu.VMEM((lines, rows, width), jnp.bfloat16),
            pltpu.VMEM((members, SUBLANES, LANES), f32),
            pltpu.VMEM((lines, SUBLANES, LANES), f32),
            pltpu.VMEM((rows, LANES), f32),
            pltpu.VMEM((rows, LANES), f32),
            pltpu.VMEM((members, SUBLANES, rows), f32),
            pltpu.VMEM((lines, SUBLANES, rows), f32),
            pltpu.VMEM((members, SUBLANES, rows), f32),
            pltpu.VMEM((lines, SUBLANES, rows), f32),
            pltpu.VMEM((SUBLANES, rows), f32),
            dma((members, 2)),
            dma((members, 2)),
            dma((lines, 2)),
            dma((lines, 2)),
            dma((members,)),
            dma((members,)),
            dma((lines,)),
            dma((lines,)),
            dma((members,)),
            dma((members,)),
            dma((lines,)),
            dma((lines,)),
        ],
        compiler_params=pltpu.CompilerParams(
            collective_id=0, has_side_effects=True, vmem_limit_bytes=48 * 2**20
        ),
    )(embeddings, row_target.reshape(1, rows))
    return best.reshape(rows)


def solution(mesh):
    in_specs = (P(("grp", "mem"), None), P(("grp", "mem"), None))
    return jax.shard_map(
        per_device, mesh=mesh, in_specs=in_specs, out_specs=P(("grp", "mem")), check_vma=False
    )
```

time: 62 us -> 55.8 us (0.90)
  Pallas kernels: 59.4 us -> 53.2 us
    pallas_call x1, Pallas kernels: 59.4 us -> 53.2 us  [per_device(): pl.pallas_call(functools.partial(kernel, groups, members), out_shape=jax....]
where the time goes in v2:
time: 55.8 us; the launch traced here: 55.6 us
  Pallas kernels  53.2 us (95%)
  local copies, waits for them, and re-layouts  1.81 us (3%)
  other arithmetic  0.6 us (1%)
    pallas_call x1, Pallas kernels, per_device(): pl.pallas_call(functools.partial(kernel, groups, members), out_shape=jax....  53.2 us
    unnamed x4, local copies, waits for them, and re-layouts  1.81 us

profile of v2, /device:TPU:0, one launch (start us, length us, event | category | flops | bytes accessed | tf_op | source)
XLA Modules:
  0.0 55.6 jit_solution(1864276444309121154)
XLA Ops:
  0.0 0.0 copy-start.1
  0.0 0.7 %copy-done.1 = s32[384,1]{0,1:T(1,128)S(1)} copy-done((s32[384,1]{0,1:T(1,128)S(1)}, s32[384,1]{0,1:T(1,128)}, u32[]{:S(2)}) %copy-start.1) | copy-done | bytes 1560
  0.7 0.0 copy-start
  0.7 1.1 %copy-done = bf16[384,1024]{1,0:T(8,128)(2,1)S(1)} copy-done((bf16[384,1024]{1,0:T(8,128)(2,1)S(1)}, bf16[384,1024]{1,0:T(8,128)(2,1)}, u32[]{:S(2)}) %copy-start) | copy-done | bytes 786456
  1.8 53.2 %shard_map.28 = f32[1,384]{1,0:T(1,128)S(1)} custom-call(bf16[384,1024]{1,0:T(8,128)(2,1)S(1)} %copy-done, s32[1,384]{1,0:T(1,128)S(1)} %bitcast.1), custom_call_target="tpu_custom_call" | custom-call | tf_op jit(solution)/shard_map/pallas_call | solution.py:288
  55.0 0.6 %reduce = f32[384]{0:T(512)} reduce(f32[1,384]{1,0:T(1,128)S(1)} %shard_map.28, f32[]{:T(128)} %constant), dimensions={0}, to_apply=%pallas_call.3.reduce_sub_computation | reduce | bytes 3076 | tf_op jit(solution)/shard_map/pallas_call | solution.py:288
Async XLA Ops:
  0.0 0.7 %copy-start.1 = (s32[384,1]{0,1:T(1,128)S(1)}, s32[384,1]{0,1:T(1,128)}, u32[]{:S(2)}) copy-start(s32[384,1]{0,1:T(1,128)} %param.3) | copy-start | bytes 4612
  0.7 1.1 %copy-start = (bf16[384,1024]{1,0:T(8,128)(2,1)S(1)}, bf16[384,1024]{1,0:T(8,128)(2,1)}, u32[]{:S(2)}) copy-start(bf16[384,1024]{1,0:T(8,128)(2,1)} %emb_ref.1) | copy-start | bytes 2359300

commit v3 on v2

--- a/solution.py
+++ b/solution.py
@@ -84,10 +84,16 @@
 
     pl.semaphore_wait(barrier, members - 1 + groups - 1)
 
+    def size(p):
+        return (parts[p][1] - parts[p][0]) * LANES
+
+    def base(p, j):
+        return p * lines * size(0) + j * size(p)
+
     def line_copy(j, p):
         at = pl.ds(parts[p][0] * LANES, (parts[p][1] - parts[p][0]) * LANES)
         return pltpu.make_async_remote_copy(
-            src_ref=plane.at[0, at], dst_ref=line.at[j, at],
+            src_ref=plane.at[0, at], dst_ref=line.at[pl.ds(base(p, j), size(p))],
             send_sem=line_send.at[j, p], recv_sem=line_recv.at[j, p],
             device_id=group_below(j), device_id_type=MESH,
         )
@@ -140,7 +146,7 @@
     def see(i):
         for k in range(pieces):
             row = jnp.broadcast_to(plane_tag[i, k:k + 1, :], (LANES, LANES))
-            seen[k * LANES:(k + 1) * LANES, :] = jnp.transpose(row)
+            seen[i, k * LANES:(k + 1) * LANES, :] = jnp.transpose(row)
 
     def cosines(i, left):
         return lax.dot_general(
@@ -152,11 +158,10 @@
     plane_out[...] = jnp.full((members, SUBLANES, rows), -1.0, jnp.float32)
 
     def own_pairs(i, same=False):
-        see(i)
         cos = cosines(i, plane[0])
         for k in range(pieces):
             at = pl.ds(k * LANES, LANES)
-            keep = seen[...] == plane_tag[0, k:k + 1, :]
+            keep = seen[i] == plane_tag[0, k:k + 1, :]
             if same:
                 down = lax.broadcasted_iota(jnp.int32, (rows, LANES), 0)
                 over = lax.broadcasted_iota(jnp.int32, (rows, LANES), 1) + k * LANES
@@ -164,9 +169,11 @@
             part = jnp.where(keep, cos[:, k * LANES:(k + 1) * LANES], -1.0)
             own_best[:, at] = jnp.maximum(own_best[:, at], jnp.max(part, axis=0, keepdims=True))
 
+    see(0)
     own_pairs(0, True)
     for i in range(1, members):
         tag_copy(i).wait_recv()
+        see(i)
     for j in range(lines):
         if_takes(j, lambda j=j: end_copy(j).wait_recv())
 
@@ -178,35 +185,44 @@
                 plane_copy(source, onto, h).start()
         plane_copy(slot, 1, h).start()
 
-    for h in range(2):
-        plane_copy(0, 1, h).wait_recv()
-    own_pairs(1)
-    have = 0
-    for slot, h in order:
-        arrive(slot, h)
-        if slot == 4 and h == 0 and relayed:
-            for i in (2, 4):
-                own_pairs(i)
-            have = 4
-    for i in range(2, members):
-        if i % 2:
-            for h in range(2):
-                plane_copy(i - 1, 1, h).wait_recv()
-        if not (have and i in (2, 4)):
-            own_pairs(i)
-
-    def line_pairs(j, i, p):
+    def line_pairs(i, p, count):
+        if count == 0:
+            return
         start, stop = parts[p]
-        cos = cosines(i, line[j, start * LANES:stop * LANES, :])
-        for k in range(start, stop):
-            at = pl.ds(k * LANES, LANES)
-            keep = seen[...] == line_tag[j, k:k + 1, :]
-            cut = cos[:, (k - start) * LANES:(k - start + 1) * LANES]
-            part = jnp.where(keep, cut, -1.0)
-            line_out[j, :, at] = jnp.maximum(
-                line_out[j, :, at], jnp.max(part, axis=0, keepdims=True)
-            )
-            reached[...] = jnp.maximum(reached[...], part)
+        cos = cosines(i, line[base(p, 0):base(p, count), :])
+        best = None
+        for j in range(count):
+            for k in range(start, stop):
+                at = pl.ds(k * LANES, LANES)
+                c = j * (stop - start) + k - start
+                keep = seen[i] == line_tag[j, k:k + 1, :]
+                part = jnp.where(keep, cos[:, c * LANES:(c + 1) * LANES], -1.0)
+                line_out[j, :, at] = jnp.maximum(
+                    line_out[j, :, at], jnp.max(part, axis=0, keepdims=True)
+                )
+                best = part if best is None else jnp.maximum(best, part)
+        if p == 0:
+            reached[i] = best
+        else:
+            best = jnp.transpose(jnp.maximum(best, reached[i]))
+            plane_out[i] = jnp.broadcast_to(jnp.max(best, axis=0, keepdims=True), (SUBLANES, rows))
+
+    def taken(body):
+        if has_half:
+            pl.when(takes_half)(lambda: body(lines))
+            pl.when(gives_half)(lambda: body(full))
+        else:
+            body(lines)
+
+    def first_parts(start, stop):
+        def loop(count):
+            def step(i, carry):
+                line_pairs(i, 0, count)
+                return carry
+
+            lax.fori_loop(start, stop, step, 0)
+
+        taken(loop)
 
     def back_copy(i):
         return pltpu.make_async_remote_copy(
@@ -222,26 +238,52 @@
             device_id=(lax.rem(g + steps[j], groups), m), device_id_type=MESH,
         )
 
-    def across_lines(i, p):
-        see(i)
-        reached[...] = jnp.full((rows, LANES), -1.0, jnp.float32)
-        for j in range(lines):
-            if_takes(j, lambda j=j: line_pairs(j, i, p))
-        best = jnp.max(jnp.transpose(reached[...]), axis=0, keepdims=True)
-        plane_out[i] = jnp.maximum(plane_out[i], best)
-
-    for p in range(2):
+    def wait_line(p):
         for j in range(lines):
             if_takes(j, lambda j=j, p=p: line_copy(j, p).wait_recv())
 
-        def step(i, carry, p=p):
-            across_lines(i, p)
-            if p == 1:
-                back_copy(i).start()
+    def from_partner(i):
+        for h in range(2):
+            plane_copy(i - 1, 1, h).wait_recv()
+        own_pairs(i)
+
+    from_partner(1)
+    late = 2 if relayed else 0
+    early = len(order) - late
+    for slot, h in order[:early]:
+        arrive(slot, h)
+    reach = 2 + early
+    for i in range(2, reach, 2):
+        own_pairs(i)
+    for i in range(3, reach, 2):
+        from_partner(i)
+    wait_line(0)
+    first_parts(0, 2)
+    for slot, h in order[early:]:
+        arrive(slot, h)
+    first_parts(2, reach)
+    if late:
+        own_pairs(reach)
+        first_parts(reach, reach + 1)
+        from_partner(reach + 1)
+        first_parts(reach + 1, reach + 2)
+    wait_line(1)
+
+    def last_parts(count):
+        line_pairs(0, 1, count)
+        line_pairs(1, 1, count)
+        back_copy(1).start()
+
+        def step(t, carry):
+            line_pairs(2 * t, 1, count)
+            line_pairs(2 * t + 1, 1, count)
+            back_copy(2 * t).start()
+            back_copy(2 * t + 1).start()
             return carry
 
-        lax.fori_loop(1, members, step, 0)
-        across_lines(0, p)
+        lax.fori_loop(1, members // 2, step, 0)
+
+    taken(last_parts)
 
     for j in range(lines):
         if_takes(j, lambda j=j: home_copy(j).start())
@@ -292,11 +334,11 @@
         out_specs=pl.BlockSpec(memory_space=pltpu.VMEM),
         scratch_shapes=[
             pltpu.VMEM((members, rows, width), jnp.bfloat16),
-            pltpu.VMEM((lines, rows, width), jnp.bfloat16),
+            pltpu.VMEM((lines * rows, width), jnp.bfloat16),
             pltpu.VMEM((members, SUBLANES, LANES), f32),
             pltpu.VMEM((lines, SUBLANES, LANES), f32),
-            pltpu.VMEM((rows, LANES), f32),
-            pltpu.VMEM((rows, LANES), f32),
+            pltpu.VMEM((members, rows, LANES), f32),
+            pltpu.VMEM((members, rows, LANES), f32),
             pltpu.VMEM((members, SUBLANES, rows), f32),
             pltpu.VMEM((lines, SUBLANES, rows), f32),
             pltpu.VMEM((members, SUBLANES, rows), f32),

time: 55.8 us -> 50.2 us (0.90)
  Pallas kernels: 53.2 us -> 47.7 us
    pallas_call x1, Pallas kernels: 53.2 us -> 47.7 us  [per_device(): pl.pallas_call(functools.partial(kernel, groups, members), out_shape=jax....]
where the time goes in v3:
time: 50.2 us; the launch traced here: 50.1 us
  Pallas kernels  47.7 us (95%)
  local copies, waits for them, and re-layouts  1.81 us (4%)
  other arithmetic  0.6 us (1%)
    pallas_call x1, Pallas kernels, per_device(): pl.pallas_call(functools.partial(kernel, groups, members), out_shape=jax....  47.7 us
    unnamed x4, local copies, waits for them, and re-layouts  1.81 us

profile of v3, /device:TPU:0, one launch (start us, length us, event | category | flops | bytes accessed | tf_op | source)
XLA Modules:
  0.0 50.1 jit_solution(8945436637592635258)
XLA Ops:
  0.0 0.0 copy-start.1
  0.0 0.7 %copy-done.1 = s32[384,1]{0,1:T(1,128)S(1)} copy-done((s32[384,1]{0,1:T(1,128)S(1)}, s32[384,1]{0,1:T(1,128)}, u32[]{:S(2)}) %copy-start.1) | copy-done | bytes 1560
  0.7 0.0 copy-start
  0.7 1.1 %copy-done = bf16[384,1024]{1,0:T(8,128)(2,1)S(1)} copy-done((bf16[384,1024]{1,0:T(8,128)(2,1)S(1)}, bf16[384,1024]{1,0:T(8,128)(2,1)}, u32[]{:S(2)}) %copy-start) | copy-done | bytes 786456
  1.8 47.7 %shard_map.28 = f32[1,384]{1,0:T(1,128)S(1)} custom-call(bf16[384,1024]{1,0:T(8,128)(2,1)S(1)} %copy-done, s32[1,384]{1,0:T(1,128)S(1)} %bitcast.1), custom_call_target="tpu_custom_call" | custom-call | tf_op jit(solution)/shard_map/pallas_call | solution.py:330
  49.5 0.6 %reduce = f32[384]{0:T(512)} reduce(f32[1,384]{1,0:T(1,128)S(1)} %shard_map.28, f32[]{:T(128)} %constant), dimensions={0}, to_apply=%pallas_call.3.reduce_sub_computation | reduce | bytes 3076 | tf_op jit(solution)/shard_map/pallas_call | solution.py:330
Async XLA Ops:
  0.0 0.7 %copy-start.1 = (s32[384,1]{0,1:T(1,128)S(1)}, s32[384,1]{0,1:T(1,128)}, u32[]{:S(2)}) copy-start(s32[384,1]{0,1:T(1,128)} %param.3) | copy-start | bytes 4612
  0.7 1.1 %copy-start = (bf16[384,1024]{1,0:T(8,128)(2,1)S(1)}, bf16[384,1024]{1,0:T(8,128)(2,1)}, u32[]{:S(2)}) copy-start(bf16[384,1024]{1,0:T(8,128)(2,1)} %emb_ref.1) | copy-start | bytes 2359300

commit v4 on v3

--- a/solution.py
+++ b/solution.py
@@ -72,11 +72,15 @@
             barrier, inc=1, device_id=(lax.rem(g + i, groups), m), device_id_type=MESH
         )
 
-    values = emb_ref[...].astype(jnp.float32)
-    inv_norm = lax.rsqrt(jnp.mean(values * values, axis=1, keepdims=True) + 1e-06) * (
-        1.0 / math.sqrt(width)
-    )
-    plane[0] = (values * inv_norm).astype(jnp.bfloat16)
+    def normalize(start, stop):
+        values = emb_ref[start:stop, :].astype(jnp.float32)
+        inv_norm = lax.rsqrt(jnp.mean(values * values, axis=1, keepdims=True) + 1e-06) * (
+            1.0 / math.sqrt(width)
+        )
+        plane[0, start:stop, :] = (values * inv_norm).astype(jnp.bfloat16)
+
+    cut = parts[0][1] * LANES
+    normalize(0, cut)
     cluster = jnp.floor((target_ref[...].astype(jnp.float32) + 0.5) * (1.0 / members))
     plane_tag[0] = jnp.zeros((SUBLANES, LANES), jnp.float32)
     for k in range(pieces):
@@ -130,16 +134,22 @@
     else:
         order = [(slot, h) for slot in range(2, members, 2) for h in range(2)]
 
+    first = [key for key in order if plan[key][0] == 0]
+    for j in range(lines):
+        if_gives(j, lambda j=j: line_copy(j, 0).start())
+    for slot, h in first:
+        if h == 0:
+            plane_copy(0, slot, h).start()
+    normalize(cut, rows)
+    for slot, h in first:
+        if h == 1:
+            plane_copy(0, slot, h).start()
+    for j in range(lines):
+        if_gives(j, lambda j=j: line_copy(j, 1).start())
     for i in range(1, members):
         tag_copy(i).start()
     for j in range(lines):
         if_gives(j, lambda j=j: end_copy(j).start())
-    first = [key for key in order if plan[key][0] == 0]
-    for p in range(2):
-        for h, to in [(h, to) for to, h in first[p * len(first) // 2:(p + 1) * len(first) // 2]]:
-            plane_copy(0, to, h).start()
-        for j in range(lines):
-            if_gives(j, lambda j=j, p=p: line_copy(j, p).start())
     for h in range(2):
         plane_copy(0, 1, h).start()
 

time: 50.2 us -> 65.8 us (1.31)
  Pallas kernels: 47.7 us -> 63.3 us
    pallas_call x1, Pallas kernels: 47.7 us -> 63.3 us  [per_device(): pl.pallas_call(functools.partial(kernel, groups, members), out_shape=jax....]
where the time goes in v4:
time: 65.8 us; the launch traced here: 65.7 us
  Pallas kernels  63.3 us (96%)
  local copies, waits for them, and re-layouts  1.81 us (3%)
    pallas_call x1, Pallas kernels, per_device(): pl.pallas_call(functools.partial(kernel, groups, members), out_shape=jax....  63.3 us
    unnamed x4, local copies, waits for them, and re-layouts  1.81 us

profile of v4, /device:TPU:0, one launch (start us, length us, event | category | flops | bytes accessed | tf_op | source)
XLA Modules:
  0.0 65.7 jit_solution(1369839243163950840)
XLA Ops:
  0.0 0.0 copy-start.1
  0.0 0.7 %copy-done.1 = s32[384,1]{0,1:T(1,128)S(1)} copy-done((s32[384,1]{0,1:T(1,128)S(1)}, s32[384,1]{0,1:T(1,128)}, u32[]{:S(2)}) %copy-start.1) | copy-done | bytes 1560
  0.7 0.0 copy-start
  0.7 1.1 %copy-done = bf16[384,1024]{1,0:T(8,128)(2,1)S(1)} copy-done((bf16[384,1024]{1,0:T(8,128)(2,1)S(1)}, bf16[384,1024]{1,0:T(8,128)(2,1)}, u32[]{:S(2)}) %copy-start) | copy-done | bytes 786456
  1.8 63.3 %shard_map.28 = f32[1,384]{1,0:T(1,128)S(1)} custom-call(bf16[384,1024]{1,0:T(8,128)(2,1)S(1)} %copy-done, s32[1,384]{1,0:T(1,128)S(1)} %bitcast.1), custom_call_target="tpu_custom_call" | custom-call | tf_op jit(solution)/shard_map/pallas_call | solution.py:340
  65.1 0.6 reduce
Async XLA Ops:
  0.0 0.7 %copy-start.1 = (s32[384,1]{0,1:T(1,128)S(1)}, s32[384,1]{0,1:T(1,128)}, u32[]{:S(2)}) copy-start(s32[384,1]{0,1:T(1,128)} %param.3) | copy-start | bytes 4612
  0.7 1.1 %copy-start = (bf16[384,1024]{1,0:T(8,128)(2,1)S(1)}, bf16[384,1024]{1,0:T(8,128)(2,1)}, u32[]{:S(2)}) copy-start(bf16[384,1024]{1,0:T(8,128)(2,1)} %emb_ref.1) | copy-start | bytes 2359300
